TPU v7x, 128 devices: a whole 4x4x4 slice. The times are simulated.
128 devices in a mesh: ctx: 8 (over x, core), tp: 16 (over z, y).
Axes of the slice: x: 4, y: 4, z: 4, core: 2. Of those that a mesh axis runs over, the one named last changes fastest.
Arguments:
- tokens: bfloat16 [8192, 4096], P('ctx', 'tp')
- modality: int32 [8192], P('ctx'), may hold values from 0 to 2, as said below
- w_query: bfloat16 [3, 4096, 4096], P(None, None, 'tp')
- w_key: bfloat16 [3, 4096, 4096], P(None, None, 'tp'), may hold values from -0.09375 to 0.09375
- w_value: bfloat16 [3, 4096, 4096], P(None, None, 'tp'), may hold values from -0.09375 to 0.09375
- w_out: bfloat16 [3, 4096, 4096], P(None, 'tp'), may hold values from -0.5 to 0.5
Outputs:
- mixed: bfloat16 [8192, 4096], P('ctx', 'tp')
Inputs may be any that keep to these rules, and one draw needn't show every extreme that they name: In each aligned block of 1024 tokens (one index of ctx) the tokens of each modality form one contiguous run of at most 512 tokens; in every draw some block has a modality with exactly 512 tokens.
All inputs are finite; a program needn't handle non-finite values.
Results may differ from a plain program's by a relative error of at most 0.013.
Values may be sent and summed in bfloat16 or wider, within the bound.
No kernel may reach another device: no remote copies, remote signals or barrier semaphores. Data moves between devices by JAX's collectives and lax.ppermute only.
A program may use at most 128 MiB of HBM per device.

v0:
```python
import math

import jax
import jax.numpy as jnp
from jax import lax
from jax.sharding import PartitionSpec as P

HD = 128
MODALITIES = 3
CAP = 512


def modal_product(inputs, stacked, modality):
    row_count = inputs.shape[0]
    positions = jnp.arange(row_count, dtype=jnp.int32)
    results = [jnp.zeros((row_count, weight.shape[2]), jnp.float32) for weight in stacked]
    for modal_index in range(MODALITIES):
        member = modality == modal_index
        first_row = jnp.min(jnp.where(member, positions, row_count))
        begin_row = jnp.clip(first_row, 0, row_count - CAP)
        window = lax.dynamic_slice_in_dim(inputs, begin_row, CAP, 0)
        keep_rows = lax.dynamic_slice_in_dim(member, begin_row, CAP, 0)[:, None]
        for weight_index in range(len(stacked)):
            product = jnp.dot(
                window, stacked[weight_index][modal_index], preferred_element_type=jnp.float32
            )
            former = lax.dynamic_slice_in_dim(results[weight_index], begin_row, CAP, 0)
            results[weight_index] = lax.dynamic_update_slice_in_dim(
                results[weight_index], jnp.where(keep_rows, product, former), begin_row, 0
            )
    return results


def make_fold(queries, query_pos, fold_state, pieces):
    row_count = queries.shape[0]
    head_count = queries.shape[1]
    score_scale = 1.0 / math.sqrt(HD)
    last_query = query_pos[-1]
    key_piece, value_piece = pieces
    length = key_piece.shape[0]
    block_width = min(length, max(row_count, 512))
    while length % block_width:
        block_width -= 1
    block_count = length // block_width
    key_blocks = key_piece.reshape(block_count, block_width, head_count, HD)
    value_blocks = value_piece.reshape(block_count, block_width, head_count, HD)
    block_starts = jnp.arange(block_count, dtype=jnp.int32) * block_width

    def fold_step(carried, block_item):
        key_block, value_block, block_start = block_item

        def attend(current):
            running_top, running_total, summed = current
            scores = (
                jnp.einsum("qhd,khd->hqk", queries, key_block, preferred_element_type=jnp.float32)
                * score_scale
            )
            key_pos = block_start + jnp.arange(block_width, dtype=jnp.int32)
            allowed = key_pos[None, :] <= query_pos[:, None]
            scores = jnp.where(allowed[None], scores, -1e30)
            new_top = jnp.maximum(running_top, jnp.max(scores, axis=-1))
            factor = jnp.exp(running_top - new_top)
            weights = jnp.where(allowed[None], jnp.exp(scores - new_top[..., None]), 0.0)
            new_total = running_total * factor + jnp.sum(weights, axis=-1)
            new_summed = summed * factor[..., None] + jnp.einsum(
                "hqk,khd->hqd",
                weights.astype(jnp.bfloat16),
                value_block,
                preferred_element_type=jnp.float32,
            )
            return (new_top, new_total, new_summed)

        return (lax.cond(block_start > last_query, lambda current: current, attend, carried), None)

    result_state, _ = lax.scan(fold_step, fold_state, (key_blocks, value_blocks, block_starts))
    return result_state


def local(tokens, modality, w_query, w_key, w_value, w_out):
    row_count = tokens.shape[0]
    gathered = lax.all_gather(tokens, "tp", axis=1, tiled=True)
    widened = gathered.astype(jnp.float32)
    normed = (
        widened * lax.rsqrt(jnp.mean(widened * widened, axis=-1, keepdims=True) + 1e-05)
    ).astype(jnp.bfloat16)
    projected = modal_product(normed, [w_query, w_key, w_value], modality)
    query_rows = projected[0].astype(jnp.bfloat16)
    key_rows = projected[1].astype(jnp.bfloat16)
    value_rows = projected[2].astype(jnp.bfloat16)
    head_count = query_rows.shape[1] // HD
    queries = query_rows.reshape(row_count, head_count, HD)
    query_pos = lax.axis_index("ctx") * row_count + jnp.arange(row_count, dtype=jnp.int32)
    initial = (
        jnp.full((head_count, row_count), -1e30, jnp.float32),
        jnp.zeros((head_count, row_count), jnp.float32),
        jnp.zeros((head_count, row_count, HD), jnp.float32),
    )
    running_top, running_total, summed = make_fold(
        queries,
        query_pos,
        initial,
        (
            lax.all_gather(key_rows, "ctx", axis=0, tiled=True),
            lax.all_gather(value_rows, "ctx", axis=0, tiled=True),
        ),
    )
    attended = (
        jnp.transpose(summed / running_total[..., None], (1, 0, 2))
        .reshape(row_count, head_count * HD)
        .astype(jnp.bfloat16)
    )
    partial_term = modal_product(attended, [w_out], modality)[0]
    branch = lax.psum_scatter(
        partial_term.astype(jnp.bfloat16), "tp", scatter_dimension=1, tiled=True
    ).astype(jnp.float32)
    return (tokens.astype(jnp.float32) + branch).astype(jnp.bfloat16)


def solution(mesh):
    in_specs = (
        P("ctx", "tp"),
        P("ctx"),
        P(None, None, "tp"),
        P(None, None, "tp"),
        P(None, None, "tp"),
        P(None, "tp", None),
    )
    out_specs = P("ctx", "tp")
    return jax.shard_map(local, mesh=mesh, in_specs=in_specs, out_specs=out_specs, check_vma=False)
```

profile of v0, /device:TPU:6, one launch (start us, length us, event | category | flops | bytes accessed | tf_op | source)
XLA Modules:
  0.0 485.0 jit_solution(1685615473785368563)
XLA Ops:
  10.8 79.6 %all-gather.4.cloned.1.call-done = bf16[1024,4096]{1,0:T(8,128)(2,1)} async-done(((bf16[1024,256]{1,0:T(8,128)(2,1)}), bf16[1024,4096]{1,0:T(8,128)(2,1)}) %all-gather.4.cloned.1.call-update) | async-done | bytes 8388624 | tf_op jit(solution)/shard_map/all_gather | solution.py:81
  90.4 5.1 %fusion.21 = f32[1024]{0:T(1024)S(1)} fusion(bf16[1024,4096]{1,0:T(8,128)(2,1)} %all-gather.4.cloned.1.call-done), kind=kLoop, calls=%fused_computation.26 | loop fusion | flops 12581888 | bytes 8392704 | tf_op jit(solution)/shard_map/reduce_sum | solution.py:84
  95.5 10.0 %fusion.22 = bf16[1024,4096]{1,0:T(8,128)(2,1)} fusion(bf16[1024,4096]{1,0:T(8,128)(2,1)} %all-gather.4.cloned.1.call-done, f32[1024]{0:T(1024)S(1)} %add_rsqrt_fusion), kind=kLoop, calls=%fused_computation.27 | loop fusion | flops 12582912 | bytes 16781312 | tf_op jit(solution)/shard_map/convert_element_type | solution.py:85
  105.4 4.1 fusion.65
  109.6 1.9 dynamic_update_slice.36
  111.5 4.1 fusion.80
  115.7 1.5 dynamic_update_slice.37
  117.2 4.1 fusion.95
  121.3 1.5 dynamic_update_slice.38
  123.9 4.2 fusion.75
  128.1 1.9 dynamic_update_slice.42
  130.0 4.3 fusion.90
  134.2 1.5 dynamic_update_slice.43
  135.7 4.2 fusion.105
  139.9 1.5 dynamic_update_slice.44
  143.0 4.3 fusion.70
  147.3 1.9 dynamic_update_slice.39
  149.2 4.2 fusion.85
  153.4 1.5 dynamic_update_slice.40
  154.9 4.1 fusion.100
  159.0 1.5 dynamic_update_slice.41
  160.6 7.0 %reshape.56 = bf16[8,1024,2,128]{3,2,1,0:T(2,128)(2,1)} reshape(bf16[8192,256]{1,0:T(8,128)(2,1)} %all-gather.6.cloned.1.call-done) | data formatting | bytes 8388608 | tf_op jit(solution)/shard_map/reshape | solution.py:45
  167.6 5.1 %copy.18 = bf16[8,1024,2,128]{3,1,2,0:T(8,128)(2,1)} copy(bf16[8,1024,2,128]{3,2,1,0:T(2,128)(2,1)} %reshape.56) | data formatting | bytes 8388608
  172.7 14.8 %all-gather.8.cloned.1.call-done = bf16[8192,256]{1,0:T(8,128)(2,1)} async-done(((bf16[1024,256]{1,0:T(8,128)(2,1)}), bf16[8192,256]{1,0:T(8,128)(2,1)}) %all-gather.8.cloned.1.call-update) | async-done | bytes 4194320 | tf_op jit(solution)/shard_map/all_gather | solution.py:104
  187.5 6.9 %reshape.58 = bf16[8,1024,2,128]{3,2,1,0:T(2,128)(2,1)} reshape(bf16[8192,256]{1,0:T(8,128)(2,1)} %all-gather.8.cloned.1.call-done) | data formatting | bytes 8388608 | tf_op jit(solution)/shard_map/reshape | solution.py:46
  194.4 5.0 %copy.20 = bf16[8,1024,2,128]{3,1,2,0:T(8,128)(2,1)} copy(bf16[8,1024,2,128]{3,2,1,0:T(2,128)(2,1)} %reshape.58) | data formatting | bytes 8388608
  199.5 94.3 %while.15 = (s32[]{:T(128)}, f32[2,1024]{1,0:T(2,128)S(1)}, f32[2,1024]{1,0:T(2,128)S(1)}, f32[2,1024,128]{2,1,0:T(8,128)S(1)}, s32[8]{0:T(128)S(1)}, /*index=5*...) while((s32[]{:T(128)}, f32[2,1024]{1,0:T(2,128)S(1)}, ...), condition=%wide.region_9.10_spmd.clone, body=%wide.region_4.9_spmd.clone.sunk | while | flops 1102583808 | bytes 33187096 | solution.py:75
  201.6 11.2 %conditional.3 = (f32[2,1024]{1,0:T(2,128)S(1)}, f32[2,1024]{1,0:T(2,128)S(1)}, f32[2,1024,128]{2,1,0:T(8,128)S(1)}) conditional(s32[]{:T(128)} %convert_element_type.74, (s32[]{:T(128)}, s32[]{:T(128)}, bf16[8,1024,2,128]{3,1,2,0:T(8,128)(2,1)}, s32[]{:T(128)}, bf16[1024,2,128]{2,0,1:T(8,128)(2,1)S(1)}, /*index=5*/f32[2,1024]{1,0:T(2,128)S(1)}, ...), branch_computations={%region_5.7_spmd, %region_8.8_spmd} | conditional | flops 1102583808 | bytes 33166368 | solution.py:73
  202.9 2.9 fusion.2
  205.8 2.3 fusion.4
  208.1 4.7 fusion.8
  214.8 11.2 %conditional.3 = (f32[2,1024]{1,0:T(2,128)S(1)}, f32[2,1024]{1,0:T(2,128)S(1)}, f32[2,1024,128]{2,1,0:T(8,128)S(1)}) conditional(s32[]{:T(128)} %convert_element_type.74, (s32[]{:T(128)}, s32[]{:T(128)}, bf16[8,1024,2,128]{3,1,2,0:T(8,128)(2,1)}, s32[]{:T(128)}, bf16[1024,2,128]{2,0,1:T(8,128)(2,1)S(1)}, /*index=5*/f32[2,1024]{1,0:T(2,128)S(1)}, ...), branch_computations={%region_5.7_spmd, %region_8.8_spmd} | conditional | flops 1102583808 | bytes 33166368 | solution.py:73
  216.1 2.9 fusion.2
  219.0 2.3 fusion.4
  221.3 4.7 fusion.8
  228.0 11.2 %conditional.3 = (f32[2,1024]{1,0:T(2,128)S(1)}, f32[2,1024]{1,0:T(2,128)S(1)}, f32[2,1024,128]{2,1,0:T(8,128)S(1)}) conditional(s32[]{:T(128)} %convert_element_type.74, (s32[]{:T(128)}, s32[]{:T(128)}, bf16[8,1024,2,128]{3,1,2,0:T(8,128)(2,1)}, s32[]{:T(128)}, bf16[1024,2,128]{2,0,1:T(8,128)(2,1)S(1)}, /*index=5*/f32[2,1024]{1,0:T(2,128)S(1)}, ...), branch_computations={%region_5.7_spmd, %region_8.8_spmd} | conditional | flops 1102583808 | bytes 33166368 | solution.py:73
  229.3 2.9 fusion.2
  232.1 2.3 fusion.4
  234.4 4.7 fusion.8
  241.1 11.2 %conditional.3 = (f32[2,1024]{1,0:T(2,128)S(1)}, f32[2,1024]{1,0:T(2,128)S(1)}, f32[2,1024,128]{2,1,0:T(8,128)S(1)}) conditional(s32[]{:T(128)} %convert_element_type.74, (s32[]{:T(128)}, s32[]{:T(128)}, bf16[8,1024,2,128]{3,1,2,0:T(8,128)(2,1)}, s32[]{:T(128)}, bf16[1024,2,128]{2,0,1:T(8,128)(2,1)S(1)}, /*index=5*/f32[2,1024]{1,0:T(2,128)S(1)}, ...), branch_computations={%region_5.7_spmd, %region_8.8_spmd} | conditional | flops 1102583808 | bytes 33166368 | solution.py:73
  242.4 2.9 fusion.2
  245.3 2.3 fusion.4
  247.6 4.7 fusion.8
  254.3 11.2 %conditional.3 = (f32[2,1024]{1,0:T(2,128)S(1)}, f32[2,1024]{1,0:T(2,128)S(1)}, f32[2,1024,128]{2,1,0:T(8,128)S(1)}) conditional(s32[]{:T(128)} %convert_element_type.74, (s32[]{:T(128)}, s32[]{:T(128)}, bf16[8,1024,2,128]{3,1,2,0:T(8,128)(2,1)}, s32[]{:T(128)}, bf16[1024,2,128]{2,0,1:T(8,128)(2,1)S(1)}, /*index=5*/f32[2,1024]{1,0:T(2,128)S(1)}, ...), branch_computations={%region_5.7_spmd, %region_8.8_spmd} | conditional | flops 1102583808 | bytes 33166368 | solution.py:73
  255.6 2.9 fusion.2
  258.5 2.3 fusion.4
  260.8 4.7 fusion.8
  267.4 11.2 %conditional.3 = (f32[2,1024]{1,0:T(2,128)S(1)}, f32[2,1024]{1,0:T(2,128)S(1)}, f32[2,1024,128]{2,1,0:T(8,128)S(1)}) conditional(s32[]{:T(128)} %convert_element_type.74, (s32[]{:T(128)}, s32[]{:T(128)}, bf16[8,1024,2,128]{3,1,2,0:T(8,128)(2,1)}, s32[]{:T(128)}, bf16[1024,2,128]{2,0,1:T(8,128)(2,1)S(1)}, /*index=5*/f32[2,1024]{1,0:T(2,128)S(1)}, ...), branch_computations={%region_5.7_spmd, %region_8.8_spmd} | conditional | flops 1102583808 | bytes 33166368 | solution.py:73
  268.8 2.9 fusion.2
  271.6 2.3 fusion.4
  273.9 4.7 fusion.8
  280.6 11.2 %conditional.3 = (f32[2,1024]{1,0:T(2,128)S(1)}, f32[2,1024]{1,0:T(2,128)S(1)}, f32[2,1024,128]{2,1,0:T(8,128)S(1)}) conditional(s32[]{:T(128)} %convert_element_type.74, (s32[]{:T(128)}, s32[]{:T(128)}, bf16[8,1024,2,128]{3,1,2,0:T(8,128)(2,1)}, s32[]{:T(128)}, bf16[1024,2,128]{2,0,1:T(8,128)(2,1)S(1)}, /*index=5*/f32[2,1024]{1,0:T(2,128)S(1)}, ...), branch_computations={%region_5.7_spmd, %region_8.8_spmd} | conditional | flops 1102583808 | bytes 33166368 | solution.py:73
  281.9 2.9 fusion.2
  284.8 2.3 fusion.4
  287.1 4.7 fusion.8
  294.3 5.0 %convolution_select_fusion = bf16[512,4096]{1,0:T(8,128)(2,1)} fusion(pred[512]{0:T(512)(128)(4,1)S(1)} %dynamic_slice.78, bf16[3,256,4096]{2,1,0:T(8,128)(2,1)} %param.15, bf16[1024,256]{0,1:T(8,128)(2,1)S(1)} %bitcast.90, s32[]{:T(128)S(6)} %min.13), kind=kOutput, calls=%fused_computation.30 | convolution fusion | flops 1075838976 | bytes 6554116 | tf_op jit(solution)/shard_map/dot_general | solution.py:24
  299.3 4.3 broadcast_in_dim.114
  303.5 21.0 %dynamic_update_slice.45 = bf16[1024,4096]{1,0:T(8,128)(2,1)} dynamic-update-slice(bf16[1024,4096]{1,0:T(8,128)(2,1)} %broadcast_in_dim.114, bf16[512,4096]{1,0:T(8,128)(2,1)} %convolution_select_fusion, s32[]{:T(128)S(6)} %min.13, s32[]{:T(128)} %constant.57.clone.1) | dynamic-update-slice | bytes 8388612 | tf_op jit(solution)/shard_map/dynamic_update_slice | solution.py:28
  324.5 6.7 %dynamic-slice_select_fusion.1 = bf16[512,4096]{1,0:T(8,128)(2,1)} fusion(bf16[1024,4096]{1,0:T(8,128)(2,1)} %dynamic_update_slice.45, s32[]{:T(128)S(6)} %min.14, pred[512]{0:T(512)(128)(4,1)S(1)} %dynamic_slice.80, bf16[3,256,4096]{2,1,0:T(8,128)(2,1)} %param.15, bf16[1024,256]{0,1:T(8,128)(2,1)S(1)} %bitcast.91), kind=kOutput, calls=%fused_computation.29 | convolution fusion | flops 1075838976 | bytes 10749440 | tf_op jit(solution)/shard_map/dot_general | solution.py:24
  331.2 20.5 %dynamic_update_slice.46 = bf16[1024,4096]{1,0:T(8,128)(2,1)} dynamic-update-slice(bf16[1024,4096]{1,0:T(8,128)(2,1)} %dynamic_update_slice.45, bf16[512,4096]{1,0:T(8,128)(2,1)} %dynamic-slice_select_fusion.1, s32[]{:T(128)S(6)} %min.14, s32[]{:T(128)} %constant.57.clone.1) | dynamic-update-slice | bytes 8388612 | tf_op jit(solution)/shard_map/dynamic_update_slice | solution.py:28
  351.8 6.7 %dynamic-slice_select_fusion = bf16[512,4096]{1,0:T(8,128)(2,1)} fusion(bf16[1024,4096]{1,0:T(8,128)(2,1)} %dynamic_update_slice.46, s32[]{:T(128)S(6)} %min.15, pred[512]{0:T(512)(128)(4,1)S(1)} %dynamic_slice.83, bf16[3,256,4096]{2,1,0:T(8,128)(2,1)} %param.15, bf16[1024,256]{0,1:T(8,128)(2,1)S(1)} %bitcast.92), kind=kOutput, calls=%fused_computation.28 | convolution fusion | flops 1075838976 | bytes 10749440 | tf_op jit(solution)/shard_map/dot_general | solution.py:24
  358.4 20.5 %dynamic_update_slice.47 = bf16[1024,4096]{1,0:T(8,128)(2,1)} dynamic-update-slice(bf16[1024,4096]{1,0:T(8,128)(2,1)} %dynamic_update_slice.46, bf16[512,4096]{1,0:T(8,128)(2,1)} %dynamic-slice_select_fusion, s32[]{:T(128)S(6)} %min.15, s32[]{:T(128)} %constant.57.clone.1) | dynamic-update-slice | bytes 8388612 | tf_op jit(solution)/shard_map/dynamic_update_slice | solution.py:28
  379.0 97.5 %reduce-scatter.2.cloned.1.call-done = bf16[1024,256]{1,0:T(8,128)(2,1)} async-done(((bf16[1024,4096]{1,0:T(8,128)(2,1)}), bf16[1024,256]{1,0:T(8,128)(2,1)}) %reduce-scatter.2.cloned.1.call-update) | async-done | bytes 524304 | tf_op jit(solution)/shard_map/reduce_scatter | solution.py:113
  476.5 2.0 add_convert_fusion
  (86 shorter events, 19.6 us)
Async XLA Ops:
  6.5 83.9 %all-gather.4.cloned.1.call-start = ((), (), s32[]{:S(2)}) async-start(), calls=%async_computation.1 | async-start | bytes 8912896 | tf_op jit(solution)/shard_map/all_gather | solution.py:81
  7.3 153.3 %all-gather.6.cloned.1.call-start = ((), (), s32[]{:S(2)}) async-start(), calls=%async_computation.2 | async-start | bytes 4718592 | tf_op jit(solution)/shard_map/all_gather | solution.py:103
  122.8 0.8 copy-start.1
  123.6 63.9 %all-gather.8.cloned.1.call-start = ((), (), s32[]{:S(2)}) async-start(), calls=%async_computation.3 | async-start | bytes 4718592 | tf_op jit(solution)/shard_map/all_gather | solution.py:104
  141.4 0.8 copy-start.2
  142.3 334.3 %reduce-scatter.2.cloned.1.call-start = ((), (), s32[]{:S(2)}) async-start(), calls=%async_computation.4 | async-start | bytes 8912896 | tf_op jit(solution)/shard_map/reduce_scatter | solution.py:113
  379.0 97.6 %copy-start = (bf16[1024,256]{1,0:T(8,128)(2,1)S(1)}, bf16[1024,256]{1,0:T(8,128)(2,1)}, u32[]{:S(2)}) copy-start(bf16[1024,256]{1,0:T(8,128)(2,1)} %param.10) | copy-start | bytes 1572868
Sparse Core Ops, SparseCore 0:
  9.5 80.8 all-gather.3
  123.7 29.8 all-gather.5
  155.4 32.0 all-gather.7
  379.1 97.3 reduce-scatter.1
where the time goes:
time: 488 us; the launch traced here: 485 us
  waiting for transfers between devices  193 us (40%)
  local copies, waits for them, and re-layouts  113 us (23%)
  matrix products  109 us (22%)
  other arithmetic  43.4 us (9%)
  between operations  15.3 us (3%)
  loops' own time  11.4 us (2%)
    reduce_scatter x1, waiting for transfers between devices, local(): lax.psum_scatter(partial_term.astype(jnp.bfloat16), 'tp', scatter_dimensi...  97.5 us
    all_gather x1, waiting for transfers between devices, local(): gathered = lax.all_gather(tokens, 'tp', axis=1, tiled=True)  79.6 us
    dynamic_update_slice x12, local copies, waits for them, and re-layouts, modal_product(): lax.dynamic_update_slice_in_dim(results[weight_index], jnp.where(keep_row...  76.7 us
    dot_general x12, matrix products, modal_product(): jnp.dot(window, stacked[weight_index][modal_index], preferred_element_typ...  55.9 us
    dot_general x7, matrix products, attend(): jnp.einsum('hqk,khd->hqd', weights.astype(jnp.bfloat16), value_block, pre...  33.2 us
    dot_general x7, matrix products, attend(): jnp.einsum('qhd,khd->hqk', queries, key_block, preferred_element_type=jnp...  20 us
    reduce_sum x7, other arithmetic, attend(): new_total = running_total * factor + jnp.sum(weights, axis=-1)  15.8 us
    all_gather x1, waiting for transfers between devices, local(): lax.all_gather(value_rows, 'ctx', axis=0, tiled=True)  14.8 us
  transfers between devices with their start and end apart: 4, of which 3 were waited for; matrix products, arithmetic and copies ran while one was open for 10% of the time, Pallas kernels for 0%

commit v1 on v0

v1 whole, which is shorter than its diff:
```python
import functools
import math

import jax
import jax.numpy as jnp
import numpy as np
from jax import lax
from jax.experimental import pallas as pl
from jax.experimental.pallas import tpu as pltpu
from jax.sharding import PartitionSpec as P

HD = 128
MODALITIES = 3
EPS = 1e-05
ROW_TILE = 256
Q_TILE = 512
K_TILE = 512
AXES = ("ctx", "tp")
BF = jnp.bfloat16
F32 = jnp.float32
OFFSETS = np.array([0, 3, 1, 2])
VMEM_BYTES = 48 * 1024 * 1024


def plane_perm(first, step):
    pairs = []
    for ctx in range(8):
        for z in range(4):
            for y in range(4):
                along_y = (ctx % 2 == 0) == first
                to_z = z if along_y else (z + step) % 4
                to_y = (y + step) % 4 if along_y else y
                pairs.append((ctx * 16 + z * 4 + y, ctx * 16 + to_z * 4 + to_y))
    return pairs


def move(array, first, step):
    return lax.ppermute(array, AXES, plane_perm(first, step))


def move_x(array, step):
    pairs = [(x * 2 + c, ((x + step) % 4) * 2 + c) for x in range(4) for c in range(2)]
    return lax.ppermute(array, "ctx", pairs)


def swap_core(array):
    return lax.ppermute(array, "ctx", [(i, i ^ 1) for i in range(8)])


def shard_table(first_offsets, second_offsets):
    core = lax.axis_index("ctx") % 2
    tp = lax.axis_index("tp")
    z, y = tp // 4, tp % 4
    first_offsets = jnp.asarray(first_offsets, jnp.int32)
    second_offsets = jnp.asarray(second_offsets, jnp.int32)
    first = (jnp.where(core == 0, y, z) + first_offsets) % 4
    second = (jnp.where(core == 0, z, y) + second_offsets) % 4
    return jnp.where(core == 0, second * 4 + first, first * 4 + second).astype(jnp.int32)


def segment_scalars(modality):
    rows = modality.shape[0]
    kinds = jnp.arange(MODALITIES, dtype=jnp.int32)[:, None]
    member = modality[None, :] == kinds
    positions = jnp.arange(rows, dtype=jnp.int32)[None, :]
    begin = jnp.min(jnp.where(member, positions, rows), axis=1)
    end = jnp.max(jnp.where(member, positions + 1, 0), axis=1)
    end = jnp.maximum(end, begin)
    core = lax.axis_index("ctx") % 2
    return jnp.concatenate([begin, end, core[None]]).astype(jnp.int32)


def for_tiles(seg_ref, body):
    for kind in range(MODALITIES):
        begin = seg_ref[kind]
        end = seg_ref[MODALITIES + kind]

        def step(tile, carry, kind=kind, begin=begin, end=end):
            row = pl.multiple_of(tile * ROW_TILE, ROW_TILE)
            positions = row + lax.broadcasted_iota(jnp.int32, (ROW_TILE, 1), 0)
            body(kind, row, (positions >= begin) & (positions < end))
            return carry

        lax.fori_loop(begin // ROW_TILE, (end + ROW_TILE - 1) // ROW_TILE, step, 0)


def project(pieces, scale, weights, table, seg, before=None, last=False):
    counts = [piece.shape[0] for piece in pieces]
    starts = [sum(counts[:i]) for i in range(len(counts))]
    steps = sum(counts)
    rows, width = pieces[0].shape[1:]
    out_width = 3 * width
    has_before = before is not None

    def kernel(table_ref, seg_ref, *refs):
        piece_refs = refs[: len(pieces)]
        refs = refs[len(pieces) :]
        scale_ref, *refs = refs
        weight_refs = refs[:3]
        refs = refs[3:]
        if has_before:
            before_ref, *refs = refs
        if last:
            query_ref, kv_ref, query_send_ref, kv_send_ref, total, normed = refs
        else:
            total, normed = refs
        step = pl.program_id(0)

        @pl.when(step == 0)
        def _():
            total[...] = before_ref[...] if has_before else jnp.zeros_like(total)

        for piece_ref, start, count in zip(piece_refs, starts, counts):

            @pl.when((step >= start) & (step < start + count))
            def _(piece_ref=piece_ref):
                normed[...] = (piece_ref[0].astype(F32) * scale_ref[...]).astype(BF)

        def tile(kind, row, keep):
            at = pl.ds(row, ROW_TILE)
            left = jnp.where(keep, normed[at, :], jnp.zeros((), BF))
            for i in range(3):
                total[at, i * width : (i + 1) * width] += jnp.dot(
                    left, weight_refs[i][kind, 0], preferred_element_type=F32
                )

        for_tiles(seg_ref, tile)

        if last:

            @pl.when(step == steps - 1)
            def _():
                query_scale = math.log2(math.e) / math.sqrt(HD)
                core = seg_ref[2 * MODALITIES]
                for mine in range(2):

                    @pl.when(core == mine)
                    def _(mine=mine):
                        for head, q_out, kv_out in (
                            (mine, query_ref, kv_ref),
                            (1 - mine, query_send_ref, kv_send_ref),
                        ):
                            at = head * HD
                            q_out[...] = (total[:, at : at + HD] * query_scale).astype(BF)
                            kv_out[:, :HD] = total[:, width + at : width + at + HD].astype(BF)
                            kv_out[:, HD:] = total[
                                :, 2 * width + at : 2 * width + at + HD
                            ].astype(BF)

    def piece_spec(start, count):
        return pl.BlockSpec(
            (1, rows, width), lambda k, t, s: (jnp.clip(k - start, 0, count - 1), 0, 0)
        )

    whole = lambda shape: pl.BlockSpec(shape, lambda k, t, s: (0,) * len(shape))
    in_specs = [piece_spec(start, count) for start, count in zip(starts, counts)]
    in_specs.append(whole((rows, 1)))
    weight_views = [w.reshape(MODALITIES, 16, width, width) for w in weights]
    in_specs += [
        pl.BlockSpec((MODALITIES, 1, width, width), lambda k, t, s: (0, t[k], 0, 0))
    ] * 3
    operands = [*pieces, scale, *weight_views]
    if has_before:
        in_specs.append(whole((rows, out_width)))
        operands.append(before)
    scratch = [pltpu.VMEM((rows, width), BF)]
    if last:
        shapes = [(rows, HD), (rows, 2 * HD)] * 2
        out_shape = tuple(jax.ShapeDtypeStruct(shape, BF) for shape in shapes)
        out_specs = tuple(whole(shape) for shape in shapes)
        scratch = [pltpu.VMEM((rows, out_width), F32)] + scratch
    else:
        out_shape = jax.ShapeDtypeStruct((rows, out_width), F32)
        out_specs = whole((rows, out_width))
    return pl.pallas_call(
        kernel,
        grid_spec=pltpu.PrefetchScalarGridSpec(
            num_scalar_prefetch=2,
            grid=(steps,),
            in_specs=in_specs,
            out_specs=out_specs,
            scratch_shapes=scratch,
        ),
        out_shape=out_shape,
        compiler_params=pltpu.CompilerParams(vmem_limit_bytes=VMEM_BYTES),
        cost_estimate=pl.CostEstimate(
            flops=2 * steps * rows * 3 * width * width * 3 // 2,
            bytes_accessed=steps * (rows * width * 2 + 9 * width * width * 2),
            transcendentals=0,
        ),
    )(table, seg, *operands)


def fold(query, key, value, keep, state):
    top, total, summed = state
    scores = lax.dot_general(
        query, key, (((1,), (1,)), ((), ())), preferred_element_type=F32
    )
    if keep is not None:
        scores = jnp.where(keep, scores, -1e30)
    new_top = jnp.maximum(top, jnp.max(scores, axis=-1, keepdims=True))
    factor = jnp.exp2(top - new_top)
    weights = jnp.exp2(scores - new_top)
    total = total * factor + jnp.sum(weights, axis=-1, keepdims=True)
    summed = summed * factor + jnp.dot(
        weights.astype(BF), value, preferred_element_type=F32
    )
    return new_top, total, summed


def store_state(state, state_ref):
    top, total, summed = state
    state_ref[0, :, :HD] = summed
    lanes = lax.broadcasted_iota(jnp.int32, (summed.shape[0], HD), 1)
    state_ref[0, :, HD:] = jnp.where(lanes < HD // 2, top, total)


def load_state(state_ref):
    return (
        state_ref[0, :, HD : HD + 1],
        state_ref[0, :, HD + HD // 2 : HD + HD // 2 + 1],
        state_ref[0, :, :HD],
    )


def attend_own(query, kv, core):
    _, rows, _ = query.shape
    per_block = rows // Q_TILE

    def kernel(core_ref, query_ref, kv_ref, state_ref):
        place = pl.program_id(0)
        q = query_ref[0]

        def part(tile):
            block = (tile // per_block) ^ core_ref[0]
            at = pl.ds(pl.multiple_of((tile % per_block) * K_TILE, K_TILE), K_TILE)
            return kv_ref[block, at, :HD], kv_ref[block, at, HD:]

        state = (
            jnp.full((Q_TILE, 1), -1e30, F32),
            jnp.zeros((Q_TILE, 1), F32),
            jnp.zeros((Q_TILE, HD), F32),
        )
        causal = lax.broadcasted_iota(
            jnp.int32, (Q_TILE, K_TILE), 1
        ) <= lax.broadcasted_iota(jnp.int32, (Q_TILE, K_TILE), 0)
        state = fold(q, *part(place), causal, state)
        state = lax.fori_loop(
            0, place, lambda tile, state: fold(q, *part(tile), None, state), state
        )
        store_state(state, state_ref)

    at_tile = lambda i, core: ((i // per_block) ^ core[0], i % per_block, 0)
    return pl.pallas_call(
        kernel,
        grid_spec=pltpu.PrefetchScalarGridSpec(
            num_scalar_prefetch=1,
            grid=(2 * per_block,),
            in_specs=[
                pl.BlockSpec((1, Q_TILE, HD), at_tile),
                pl.BlockSpec((2, rows, 2 * HD), lambda i, core: (0, 0, 0)),
            ],
            out_specs=pl.BlockSpec((1, Q_TILE, 2 * HD), at_tile),
        ),
        out_shape=jax.ShapeDtypeStruct((2, rows, 2 * HD), F32),
        compiler_params=pltpu.CompilerParams(vmem_limit_bytes=VMEM_BYTES),
        cost_estimate=pl.CostEstimate(
            flops=10 * Q_TILE * K_TILE * HD * 4, bytes_accessed=4 << 20, transcendentals=10 * Q_TILE * K_TILE
        ),
    )(core, query, kv)


def attend_other(query, state, sources, use, last=False):
    blocks, rows, _ = query.shape
    per_block = rows // Q_TILE

    def kernel(use_ref, query_ref, before_ref, *refs):
        source_refs = refs[: len(sources)]
        out_ref, after = refs[len(sources) :]
        q = query_ref[0]
        after[...] = before_ref[...]
        for i, source_ref in enumerate(source_refs):

            @pl.when(use_ref[i] != 0)
            def _(source_ref=source_ref):
                state = load_state(after)
                for block in range(source_ref.shape[0]):
                    for tile in range(source_ref.shape[1] // K_TILE):
                        at = pl.ds(tile * K_TILE, K_TILE)
                        state = fold(
                            q, source_ref[block, at, :HD], source_ref[block, at, HD:], None, state
                        )
                store_state(state, after)

        if last:
            _, total, summed = load_state(after)
            out_ref[0] = (summed / total).astype(BF)
        else:
            out_ref[...] = after[...]

    at_tile = lambda i, use: (i // per_block, i % per_block, 0)
    out_width = HD if last else 2 * HD
    keys = sum(source.shape[0] * source.shape[1] for source in sources)
    return pl.pallas_call(
        kernel,
        grid_spec=pltpu.PrefetchScalarGridSpec(
            num_scalar_prefetch=1,
            grid=(blocks * per_block,),
            in_specs=[
                pl.BlockSpec((1, Q_TILE, HD), at_tile),
                pl.BlockSpec((1, Q_TILE, 2 * HD), at_tile),
            ]
            + [pl.BlockSpec(source.shape, lambda i, use: (0, 0, 0)) for source in sources],
            out_specs=pl.BlockSpec((1, Q_TILE, out_width), at_tile),
            scratch_shapes=[pltpu.VMEM((1, Q_TILE, 2 * HD), F32)],
        ),
        out_shape=jax.ShapeDtypeStruct((blocks, rows, out_width), BF if last else F32),
        compiler_params=pltpu.CompilerParams(vmem_limit_bytes=VMEM_BYTES),
        cost_estimate=pl.CostEstimate(
            flops=blocks * rows * keys * HD * 4,
            bytes_accessed=6 << 20,
            transcendentals=blocks * rows * keys,
        ),
    )(use, query, state, *sources)


def output_part(own, other, w_out, table, seg, adds=(), split=False):
    steps = table.shape[0]
    rows = own.shape[0]
    width = 2 * HD

    def kernel(table_ref, seg_ref, own_ref, other_ref, weight_ref, *refs):
        add_refs = refs[: len(adds)]
        *out_refs, attended, total = refs[len(adds) :]
        step = pl.program_id(0)

        @pl.when(step == 0)
        def _():
            core = seg_ref[2 * MODALITIES]

            @pl.when(core == 0)
            def _():
                attended[:, :HD] = own_ref[...]
                attended[:, HD:] = other_ref[...]

            @pl.when(core == 1)
            def _():
                attended[:, :HD] = other_ref[...]
                attended[:, HD:] = own_ref[...]

        total[...] = jnp.zeros_like(total)

        def tile(kind, row, keep):
            at = pl.ds(row, ROW_TILE)
            left = jnp.where(keep, attended[at, :], jnp.zeros((), BF))
            total[at, :] += jnp.dot(left, weight_ref[kind], preferred_element_type=F32)

        for_tiles(seg_ref, tile)
        for (array, start), add_ref in zip(adds, add_refs):

            @pl.when((step >= start) & (step < start + array.shape[0]))
            def _(add_ref=add_ref):
                total[...] += add_ref[0].astype(F32)

        if split:
            for i, out_ref in enumerate(out_refs):

                @pl.when(step == i)
                def _(out_ref=out_ref):
                    out_ref[...] = total[...].astype(BF)

        else:
            out_refs[0][0] = total[...].astype(BF)

    def add_spec(array, start):
        return pl.BlockSpec(
            (1, rows, width), lambda k, t, s: (jnp.clip(k - start, 0, array.shape[0] - 1), 0, 0)
        )

    if split:
        out_shape = (jax.ShapeDtypeStruct((rows, width), BF),) * steps
        out_specs = (pl.BlockSpec((rows, width), lambda k, t, s: (0, 0)),) * steps
    else:
        out_shape = jax.ShapeDtypeStruct((steps, rows, width), BF)
        out_specs = pl.BlockSpec((1, rows, width), lambda k, t, s: (k, 0, 0))
    return pl.pallas_call(
        kernel,
        grid_spec=pltpu.PrefetchScalarGridSpec(
            num_scalar_prefetch=2,
            grid=(steps,),
            in_specs=[
                pl.BlockSpec((rows, HD), lambda k, t, s: (0, 0)),
                pl.BlockSpec((rows, HD), lambda k, t, s: (0, 0)),
                pl.BlockSpec((MODALITIES, width, width), lambda k, t, s: (0, 0, t[k])),
            ]
            + [add_spec(array, start) for array, start in adds],
            out_specs=out_specs,
            scratch_shapes=[pltpu.VMEM((rows, width), BF), pltpu.VMEM((rows, width), F32)],
        ),
        out_shape=out_shape,
        compiler_params=pltpu.CompilerParams(vmem_limit_bytes=VMEM_BYTES),
        cost_estimate=pl.CostEstimate(
            flops=3 * steps * rows * width * width,
            bytes_accessed=steps * (3 * width * width + rows * width) * 2,
            transcendentals=0,
        ),
    )(table, seg, own, other, w_out, *[array for array, _ in adds])


def local(tokens, modality, w_query, w_key, w_value, w_out):
    seg = segment_scalars(modality)
    core = seg[2 * MODALITIES :]

    near = [tokens, move(tokens, True, 1), move(tokens, True, -1), move(tokens, True, 2)]
    group = jnp.stack(near)
    squares = jnp.sum(jnp.square(group.astype(F32)), axis=(0, 2))
    mean = (
        squares + move(squares, False, 1) + move(squares, False, -1) + move(squares, False, 2)
    ) / 4096.0
    scale = lax.rsqrt(mean + EPS)[:, None]
    from_before = move(group, False, 1)
    from_after = move(group, False, -1)
    far_low = move(from_before[:2], False, 1)
    far_high = move(from_after[2:], False, -1)
    weights = (w_query, w_key, w_value)
    table = shard_table(np.tile(OFFSETS, 4), np.repeat(OFFSETS, 4))
    partial = project([group, from_before, from_after], scale, weights, table[:12], seg)
    query, kv, query_send, kv_send = project(
        [far_low, far_high], scale, weights, table[12:], seg, before=partial, last=True
    )

    kv = jnp.stack([kv, swap_core(kv_send)])
    query = jnp.stack([query, swap_core(query_send)])
    kv_before = move_x(kv, 1)
    kv_after = move_x(kv, -1)
    kv_far_low = move_x(kv_before[:1], 1)
    kv_far_high = move_x(kv_after[1:], -1)
    chip = lax.axis_index("ctx") // 2
    state = attend_own(query, kv, core)
    near_use = jnp.stack([chip >= 1, chip == 3]).astype(jnp.int32)
    state = attend_other(query, state, [kv_before, kv_after], near_use)
    far_use = jnp.stack([chip >= 2, chip >= 2]).astype(jnp.int32)
    attended = attend_other(query, state, [kv_far_low, kv_far_high], far_use, last=True)
    own = attended[0]
    other = swap_core(attended[1])

    part = functools.partial(output_part, own, other, w_out)
    seconds = np.arange(4)
    groups = [shard_table(np.full(4, offset), seconds) for offset in range(4)]
    low = move(part(groups[2][:2], seg), True, 1)
    high = move(part(groups[2][2:], seg), True, -1)
    from_before = move(part(groups[1], seg, adds=[(low, 0)]), True, 1)
    from_after = move(part(groups[3], seg, adds=[(high, 2)]), True, -1)
    here, plus, two, minus = part(
        groups[0], seg, adds=[(from_before, 0), (from_after, 0)], split=True
    )
    branch = (
        here.astype(F32)
        + move(plus, False, 1).astype(F32)
        + move(two, False, 2).astype(F32)
        + move(minus, False, -1).astype(F32)
    )
    return (tokens.astype(F32) + branch).astype(BF)


def solution(mesh):
    in_specs = (
        P("ctx", "tp"),
        P("ctx"),
        P(None, None, "tp"),
        P(None, None, "tp"),
        P(None, None, "tp"),
        P(None, "tp", None),
    )
    return jax.shard_map(
        local, mesh=mesh, in_specs=in_specs, out_specs=P("ctx", "tp"), check_vma=False
    )
```

time: 488 us -> 312 us (0.64)
  Pallas kernels: 0 us -> 149 us
  matrix products: 109 us -> 0 us
  local copies, waits for them, and re-layouts: 113 us -> 8.64 us
  waiting for transfers between devices: 193 us -> 118 us
  other arithmetic: 43.4 us -> 4.3 us
  starting transfers between devices: 0.31 us -> 31.2 us
  between operations: 15.3 us -> 0.19 us
  loops' own time: 11.4 us -> 0 us
    pallas_call x0 -> x10, Pallas kernels: none -> 149 us  [the longest x2 69.9 us: attend_other(): pl.pallas_call(kernel, grid_spec=pltpu.PrefetchScalarGridSpec(num_scalar_...]
    ppermute x0 -> x24, waiting for transfers between devices: none -> 118 us  [the longest x17 93.1 us: move(): return lax.ppermute(array, AXES, plane_perm(first, step))]
    dot_general x26 -> x0, matrix products: 109 us -> none  [the longest x12 55.9 us: modal_product(): jnp.dot(window, stacked[weight_index][modal_index], preferred_element_typ...]
    reduce_scatter x1 -> x0, waiting for transfers between devices: 97.5 us -> none  [local(): lax.psum_scatter(partial_term.astype(jnp.bfloat16), 'tp', scatter_dimensi...]
    all_gather x3 -> x0, waiting for transfers between devices: 94.4 us -> none  [the longest x1 79.6 us: local(): gathered = lax.all_gather(tokens, 'tp', axis=1, tiled=True)]
    dynamic_update_slice x12 -> x0, local copies, waits for them, and re-layouts: 76.7 us -> none  [modal_product(): lax.dynamic_update_slice_in_dim(results[weight_index], jnp.where(keep_row...]
    ppermute x0 -> x24, starting transfers between devices: none -> 31.2 us  [the longest x17 26.7 us: move(): return lax.ppermute(array, AXES, plane_perm(first, step))]
    reduce_sum x8 -> x1, other arithmetic: 20.9 us -> 1.55 us  [local(): squares = jnp.sum(jnp.square(group.astype(F32)), axis=(0, 2))]
  transfers between devices with their start and end apart: 4 -> 24, of which waited for: 3 -> 15; matrix products, arithmetic and copies ran while one was open for 10% -> 2% of each run, Pallas kernels for 0% -> 32%
where the time goes in v1:
time: 312 us
  Pallas kernels  149 us (48%)
  waiting for transfers between devices  118 us (38%)
  starting transfers between devices  31.2 us (10%)
  local copies, waits for them, and re-layouts  8.64 us (3%)
  other arithmetic  4.3 us (1%)
    ppermute x17, waiting for transfers between devices, move(): return lax.ppermute(array, AXES, plane_perm(first, step))  93.1 us
    pallas_call x2, Pallas kernels, attend_other(): pl.pallas_call(kernel, grid_spec=pltpu.PrefetchScalarGridSpec(num_scalar_...  69.9 us
    pallas_call x2, Pallas kernels, project(): pl.pallas_call(kernel, grid_spec=pltpu.PrefetchScalarGridSpec(num_scalar_...  39.7 us
    pallas_call x5, Pallas kernels, output_part(): pl.pallas_call(kernel, grid_spec=pltpu.PrefetchScalarGridSpec(num_scalar_...  32.8 us
    ppermute x17, starting transfers between devices, move(): return lax.ppermute(array, AXES, plane_perm(first, step))  26.7 us
    ppermute x4, waiting for transfers between devices, move_x(): return lax.ppermute(array, 'ctx', pairs)  20.3 us
    pallas_call x1, Pallas kernels, attend_own(): pl.pallas_call(kernel, grid_spec=pltpu.PrefetchScalarGridSpec(num_scalar_...  6.66 us
  transfers between devices with their start and end apart: 24, of which 15 were waited for; matrix products, arithmetic and copies ran while one was open for 2% of the time, Pallas kernels for 32%

profile of v1, /device:TPU:6, one launch (start us, length us, event | category | flops | bytes accessed | tf_op | source)
XLA Modules:
  0.0 311.9 jit_solution(15386227016687778664)
XLA Ops:
  0.0 1.6 collective-permute-start
  1.6 1.7 collective-permute-start.1
  3.2 2.0 collective-permute-start.2
  5.2 5.4 %collective-permute-done = bf16[1024,256]{1,0:T(8,128)(2,1)S(1)} collective-permute-done((bf16[1024,256]{1,0:T(8,128)(2,1)}, bf16[1024,256]{1,0:T(8,128)(2,1)S(1)}, u32[]{:S(2)}, u32[]{:S(2)}) %collective-permute-start) | collective-permute-done | bytes 524320 | tf_op jit(solution)/shard_map/ppermute | solution.py:38
  10.6 0.4 collective-permute-done.1
  11.0 6.5 %collective-permute-done.2 = bf16[1024,256]{1,0:T(8,128)(2,1)S(1)} collective-permute-done((bf16[1024,256]{1,0:T(8,128)(2,1)}, bf16[1024,256]{1,0:T(8,128)(2,1)S(1)}, u32[]{:S(2)}, u32[]{:S(2)}) %collective-permute-start.2) | collective-permute-done | bytes 524320 | tf_op jit(solution)/shard_map/ppermute | solution.py:38
  17.5 1.5 multiply_reduce_fusion
  19.0 2.0 collective-permute-start.3
  21.0 2.2 collective-permute-start.5
  23.2 0.0 copy-start.4
  23.2 24.0 %collective-permute-done.3.refs_1_ = bf16[4,1024,256]{2,1,0:T(8,128)(2,1)} collective-permute-done((bf16[4,1024,256]{2,1,0:T(8,128)(2,1)S(1)}, bf16[4,1024,256]{2,1,0:T(8,128)(2,1)}, u32[]{:S(2)}, u32[]{:S(2)}) %collective-permute-start.3) | collective-permute-done | bytes 2097184 | tf_op jit(solution)/shard_map/ppermute | solution.py:38
  47.2 2.4 slice.40
  49.6 0.0 collective-permute-start.4
  49.6 0.0 collective-permute-done.5.refs_2_
  49.6 2.3 slice.41
  51.9 3.2 %collective-permute-start.6 = (bf16[2,1024,256]{2,1,0:T(8,128)(2,1)}, bf16[2,1024,256]{2,1,0:T(8,128)(2,1)}, u32[]{:S(2)}, u32[]{:S(2)}) collective-permute-start(bf16[2,1024,256]{2,1,0:T(8,128)(2,1)} %slice.41), channel_id=1, source_target_pairs={{0,12},{1,13},{2,14},{3,15},{4,0},{5,1},{6,2},{7,3},{8,4},{9,5},{1... | collective-permute-start | bytes 3145736 | tf_op jit(solution)/shard_map/ppermute | solution.py:38
  55.1 0.2 select_reduce_fusion.1
  55.3 0.1 collective-permute-start.7
  55.4 3.2 %collective-permute-start.8 = (f32[1024]{0:T(1024)S(1)}, f32[1024]{0:T(1024)S(1)}, u32[]{:S(2)}, u32[]{:S(2)}) collective-permute-start(f32[1024]{0:T(1024)S(1)} %get-tuple-element.23), channel_id=1, source_target_pairs={{0,12},{1,13},{2,14},{3,15},{4,0},{5,1},{6,2},{7,3},{8,4},{9,5},{1... | collective-permute-start | bytes 12296 | tf_op jit(solution)/shard_map/ppermute | solution.py:38
  58.6 0.1 pad_add_fusion.seg_ref
  58.7 0.1 slice.30.table_ref
  58.7 7.2 %collective-permute-done.7 = f32[1024]{0:T(1024)S(1)} collective-permute-done((f32[1024]{0:T(1024)S(1)}, f32[1024]{0:T(1024)S(1)}, u32[]{:S(2)}, u32[]{:S(2)}) %collective-permute-start.7) | collective-permute-done | bytes 4128 | tf_op jit(solution)/shard_map/ppermute | solution.py:38
  65.9 1.9 collective-permute-done.8
  67.8 0.2 copy.20.refs_3_.refs_2_
  68.0 27.6 %shard_map.154.refs_6_ = f32[1024,768]{1,0:T(8,128)} custom-call(s32[12]{0:T(128)S(1)} %bitcast.23, s32[7]{0:T(128)S(1)} %pad_add_fusion.seg_ref, bf16[4,1024,256]{2,1,0:T(8,128)(2,1)S(1)} %get-tuple-element.24.refs_0_, bf16[4,1024,256]{2,1,0:T(8,128)(2,1)} %collective-permute-done.3.refs_1_, bf16[4,1024,256]{2,1,0:T(8,128)(2,1)} %collective-permute-done.5.refs_2_, ...), custom_call_target="tpu_custom_call" | custom-call | flops 7247757312 | bytes 20447232 | tf_op jit(solution)/shard_map/pallas_call | solution.py:175
  95.6 12.1 %shard_map.155 = (bf16[1024,128]{1,0:T(8,128)(2,1)S(1)}, bf16[1024,256]{1,0:T(8,128)(2,1)S(1)}, bf16[1024,128]{1,0:T(8,128)(2,1)}, bf16[1024,256]{1,0:T(8,128)(2,1)S(1)}) custom-call(s32[4]{0:T(128)S(1)} %slice.30.table_ref, s32[7]{0:T(128)S(1)} %pad_add_fusion.seg_ref, bf16[2,1024,256]{2,1,0:T(8,128)(2,1)} %collective-permute-done.4.refs_0_, ...), custom_call_target="tpu_custom_call" | custom-call | flops 2415919104 | bytes 6815744 | tf_op jit(solution)/shard_map/pallas_call | solution.py:175
  107.7 1.9 collective-permute-done.11
  109.6 0.1 pad_maximum_fusion.1.kv_ref
  109.7 0.5 collective-permute-start.12
  110.3 1.5 collective-permute-start.13
  111.8 0.1 add_convert_fusion.1.use_ref
  111.9 0.1 add_convert_fusion.2.use_ref
  112.0 1.7 collective-permute-done.10
  113.7 1.0 pad_maximum_fusion.2.query_ref
  114.7 20.3 %collective-permute-done.12.refs_0_ = bf16[2,1024,256]{2,1,0:T(8,128)(2,1)S(1)} collective-permute-done((bf16[2,1024,256]{2,1,0:T(8,128)(2,1)S(1)}, bf16[2,1024,256]{2,1,0:T(8,128)(2,1)S(1)}, u32[]{:S(2)}, u32[]{:S(2)}) %collective-permute-start.12) | collective-permute-done | bytes 1048608 | tf_op jit(solution)/shard_map/ppermute | solution.py:43
  135.0 1.8 collective-permute-start.14
  136.8 0.6 collective-permute-start.15
  137.4 6.7 %shard_map.156.before_ref = f32[2,1024,256]{2,1,0:T(8,128)S(1)} custom-call(s32[1]{0:T(128)} %bitcast.core_ref, bf16[2,1024,128]{2,1,0:T(8,128)(2,1)S(1)} %pad_maximum_fusion.2.query_ref, bf16[2,1024,256]{2,1,0:T(8,128)(2,1)S(1)} %pad_maximum_fusion.1.kv_ref), custom_call_target="tpu_custom_call" | custom-call | flops 1342177280 | bytes 4194304 | tf_op jit(solution)/shard_map/pallas_call | solution.py:254
  144.1 1.3 copy-done.2
  145.4 44.7 %shard_map.157.before_ref = f32[2,1024,256]{2,1,0:T(8,128)S(1)} custom-call(s32[2]{0:T(128)S(1)} %add_convert_fusion.2.use_ref, bf16[2,1024,128]{2,1,0:T(8,128)(2,1)S(1)} %pad_maximum_fusion.2.query_ref, f32[2,1024,256]{2,1,0:T(8,128)} %copy-done.2, bf16[2,1024,256]{2,1,0:T(8,128)(2,1)S(1)} %collective-permute-done.12.refs_0_, ...), custom_call_target="tpu_custom_call" | custom-call | flops 4294967296 | bytes 6291456 | tf_op jit(solution)/shard_map/pallas_call | solution.py:304
  190.2 25.2 %shard_map.158 = bf16[2,1024,128]{2,1,0:T(8,128)(2,1)S(1)} custom-call(s32[2]{0:T(128)S(1)} %add_convert_fusion.1.use_ref, bf16[2,1024,128]{2,1,0:T(8,128)(2,1)S(1)} %pad_maximum_fusion.2.query_ref, f32[2,1024,256]{2,1,0:T(8,128)S(1)} %shard_map.157.before_ref, bf16[1,1024,256]{2,1,0:T(8,128)(2,1)S(1)} %collective-permute-done.14.refs_0_, ...), custom_call_target="tpu_custom_call" | custom-call | flops 2147483648 | bytes 6291456 | tf_op jit(solution)/shard_map/pallas_call | solution.py:304
  215.4 0.1 collective-permute-start.16
  215.5 0.1 fusion.3
  215.6 1.4 collective-permute-done.16.other_ref
  217.0 4.3 %shard_map.161 = bf16[2,1024,256]{2,1,0:T(8,128)(2,1)S(1)} custom-call(s32[2]{0:T(128)S(1)} %get-tuple-element.27.table_ref, s32[7]{0:T(128)S(1)} %pad_add_fusion.seg_ref, bf16[1024,128]{1,0:T(8,128)(2,1)S(1)} %get-tuple-element.26.own_ref, bf16[1024,128]{1,0:T(8,128)(2,1)S(1)} %collective-permute-done.16.other_ref, bf16[3,256,4096]{2,1,0:T(8,128)(2,1)} %weight_ref.9), custom_call_target="tpu_custom_call" | custom-call | flops 402653184 | bytes 1835008 | tf_op jit(solution)/shard_map/pallas_call | solution.py:386
  221.3 2.1 collective-permute-start.19
  223.4 5.1 %shard_map.159 = bf16[2,1024,256]{2,1,0:T(8,128)(2,1)} custom-call(s32[2]{0:T(128)S(1)} %get-tuple-element.28.table_ref, s32[7]{0:T(128)S(1)} %pad_add_fusion.seg_ref, bf16[1024,128]{1,0:T(8,128)(2,1)S(1)} %get-tuple-element.26.own_ref, bf16[1024,128]{1,0:T(8,128)(2,1)S(1)} %collective-permute-done.16.other_ref, bf16[3,256,4096]{2,1,0:T(8,128)(2,1)} %weight_ref.9), custom_call_target="tpu_custom_call" | custom-call | flops 402653184 | bytes 1835008 | tf_op jit(solution)/shard_map/pallas_call | solution.py:386
  228.4 0.0 collective-permute-start.17
  228.5 7.7 %collective-permute-done.19.refs_0_ = bf16[2,1024,256]{2,1,0:T(8,128)(2,1)S(1)} collective-permute-done((bf16[2,1024,256]{2,1,0:T(8,128)(2,1)S(1)}, bf16[2,1024,256]{2,1,0:T(8,128)(2,1)S(1)}, u32[]{:S(2)}, u32[]{:S(2)}) %collective-permute-start.19) | collective-permute-done | bytes 1048608 | tf_op jit(solution)/shard_map/ppermute | solution.py:38
  236.2 1.0 copy-done
  237.1 1.2 copy-done.1
  238.4 7.2 %shard_map.162 = bf16[4,1024,256]{2,1,0:T(8,128)(2,1)S(1)} custom-call(s32[4]{0:T(128)S(1)} %broadcast_select_fusion.1.table_ref, s32[7]{0:T(128)S(1)} %pad_add_fusion.seg_ref, bf16[1024,128]{1,0:T(8,128)(2,1)S(1)} %get-tuple-element.26.own_ref, bf16[1024,128]{1,0:T(8,128)(2,1)S(1)} %collective-permute-done.16.other_ref, bf16[3,256,4096]{2,1,0:T(8,128)(2,1)} %weight_ref.9, ...), custom_call_target="tpu_custom_call" | custom-call | flops 805306368 | bytes 3670016 | tf_op jit(solution)/shard_map/pallas_call | solution.py:386
  245.5 3.3 %collective-permute-start.20 = (bf16[4,1024,256]{2,1,0:T(8,128)(2,1)S(1)}, bf16[4,1024,256]{2,1,0:T(8,128)(2,1)}, u32[]{:S(2)}, u32[]{:S(2)}) collective-permute-start(bf16[4,1024,256]{2,1,0:T(8,128)(2,1)S(1)} %shard_map.162), channel_id=1, source_target_pairs={{0,3},{1,0},{2,1},{3,2},{4,7},{5,4},{6,5},{7,6},{8,11},{9,8},{10,9... | collective-permute-start | bytes 6291464 | tf_op jit(solution)/shard_map/ppermute | solution.py:38
  248.8 8.1 %shard_map.160 = bf16[4,1024,256]{2,1,0:T(8,128)(2,1)} custom-call(s32[4]{0:T(128)S(1)} %broadcast_select_fusion.3.table_ref, s32[7]{0:T(128)S(1)} %pad_add_fusion.seg_ref, bf16[1024,128]{1,0:T(8,128)(2,1)S(1)} %get-tuple-element.26.own_ref, bf16[1024,128]{1,0:T(8,128)(2,1)S(1)} %collective-permute-done.16.other_ref, bf16[3,256,4096]{2,1,0:T(8,128)(2,1)} %weight_ref.9, ...), custom_call_target="tpu_custom_call" | custom-call | flops 805306368 | bytes 3670016 | tf_op jit(solution)/shard_map/pallas_call | solution.py:386
  256.9 0.0 copy-start.3
  256.9 15.5 %collective-permute-done.20.refs_1_ = bf16[4,1024,256]{2,1,0:T(8,128)(2,1)} collective-permute-done((bf16[4,1024,256]{2,1,0:T(8,128)(2,1)S(1)}, bf16[4,1024,256]{2,1,0:T(8,128)(2,1)}, u32[]{:S(2)}, u32[]{:S(2)}) %collective-permute-start.20) | collective-permute-done | bytes 2097184 | tf_op jit(solution)/shard_map/ppermute | solution.py:38
  272.4 12.1 %collective-permute-done.18.refs_0_ = bf16[4,1024,256]{2,1,0:T(8,128)(2,1)} collective-permute-done((bf16[4,1024,256]{2,1,0:T(8,128)(2,1)}, bf16[4,1024,256]{2,1,0:T(8,128)(2,1)}, u32[]{:S(2)}, u32[]{:S(2)}) %collective-permute-start.18) | collective-permute-done | bytes 2097184 | tf_op jit(solution)/shard_map/ppermute | solution.py:38
  284.4 8.3 %shard_map.163 = (bf16[1024,256]{1,0:T(8,128)(2,1)S(1)}, bf16[1024,256]{1,0:T(8,128)(2,1)S(1)}, bf16[1024,256]{1,0:T(8,128)(2,1)S(1)}, bf16[1024,256]{1,0:T(8,128)(2,1)S(1)}) custom-call(s32[4]{0:T(128)S(1)} %broadcast_select_fusion.4.table_ref, s32[7]{0:T(128)S(1)} %pad_add_fusion.seg_ref, bf16[1024,128]{1,0:T(8,128)(2,1)S(1)} %get-tuple-element.26.own_ref, ...), custom_call_target="tpu_custom_call" | custom-call | flops 805306368 | bytes 3670016 | tf_op jit(solution)/shard_map/pallas_call | solution.py:386
  292.7 2.1 collective-permute-start.21
  294.8 3.1 collective-permute-start.22
  297.9 0.2 collective-permute-start.23
  298.1 5.5 %collective-permute-done.21 = bf16[1024,256]{1,0:T(8,128)(2,1)S(1)} collective-permute-done((bf16[1024,256]{1,0:T(8,128)(2,1)S(1)}, bf16[1024,256]{1,0:T(8,128)(2,1)S(1)}, u32[]{:S(2)}, u32[]{:S(2)}) %collective-permute-start.21) | collective-permute-done | bytes 524320 | tf_op jit(solution)/shard_map/ppermute | solution.py:38
  303.6 7.1 %collective-permute-done.22 = bf16[1024,256]{1,0:T(8,128)(2,1)S(1)} collective-permute-done((bf16[1024,256]{1,0:T(8,128)(2,1)S(1)}, bf16[1024,256]{1,0:T(8,128)(2,1)S(1)}, u32[]{:S(2)}, u32[]{:S(2)}) %collective-permute-start.22) | collective-permute-done | bytes 524320 | tf_op jit(solution)/shard_map/ppermute | solution.py:38
  310.7 1.2 add_convert_fusion
  (32 shorter events, 0.2 us)
Async XLA Ops:
  0.0 10.6 %collective-permute-start = (bf16[1024,256]{1,0:T(8,128)(2,1)}, bf16[1024,256]{1,0:T(8,128)(2,1)S(1)}, u32[]{:S(2)}, u32[]{:S(2)}) collective-permute-start(bf16[1024,256]{1,0:T(8,128)(2,1)} %param.16), channel_id=1, source_target_pairs={{0,1},{1,2},{2,3},{3,0},{4,5},{5,6},{6,7},{7,4},{8,9},{9,10},{10,1... | collective-permute-start | bytes 1572872 | tf_op jit(solution)/shard_map/ppermute | solution.py:38
  1.6 9.4 %collective-permute-start.1 = (bf16[1024,256]{1,0:T(8,128)(2,1)}, bf16[1024,256]{1,0:T(8,128)(2,1)S(1)}, u32[]{:S(2)}, u32[]{:S(2)}) collective-permute-start(bf16[1024,256]{1,0:T(8,128)(2,1)} %param.16), channel_id=1, source_target_pairs={{0,3},{1,0},{2,1},{3,2},{4,7},{5,4},{6,5},{7,6},{8,11},{9,8},{10,9... | collective-permute-start | bytes 1572872 | tf_op jit(solution)/shard_map/ppermute | solution.py:38
  3.2 14.2 %collective-permute-start.2 = (bf16[1024,256]{1,0:T(8,128)(2,1)}, bf16[1024,256]{1,0:T(8,128)(2,1)S(1)}, u32[]{:S(2)}, u32[]{:S(2)}) collective-permute-start(bf16[1024,256]{1,0:T(8,128)(2,1)} %param.16), channel_id=1, source_target_pairs={{0,2},{1,3},{2,0},{3,1},{4,6},{5,7},{6,4},{7,5},{8,10},{9,11},{10,... | collective-permute-start | bytes 1572872 | tf_op jit(solution)/shard_map/ppermute | solution.py:38
  17.5 5.7 %copy-start.5 = (s32[16]{0:T(128)S(1)}, s32[16]{0:T(128)}, u32[]{:S(2)}) copy-start(s32[16]{0:T(128)} %constant.166.clone) | copy-start | bytes 196
  17.5 5.7 %copy-start.6 = (s32[16]{0:T(128)S(1)}, s32[16]{0:T(128)}, u32[]{:S(2)}) copy-start(s32[16]{0:T(128)} %constant.167.clone) | copy-start | bytes 196
  19.0 28.2 %collective-permute-start.3 = (bf16[4,1024,256]{2,1,0:T(8,128)(2,1)S(1)}, bf16[4,1024,256]{2,1,0:T(8,128)(2,1)}, u32[]{:S(2)}, u32[]{:S(2)}) collective-permute-start(bf16[4,1024,256]{2,1,0:T(8,128)(2,1)S(1)} %get-tuple-element.24.refs_0_), channel_id=1, source_target_pairs={{0,4},{1,5},{2,6},{3,7},{4,8},{5,9},{6,10},{7,11},{8,12},{9,13},{1... | collective-permute-start | bytes 6291464 | tf_op jit(solution)/shard_map/ppermute | solution.py:38
  21.0 28.6 %collective-permute-start.5 = (bf16[4,1024,256]{2,1,0:T(8,128)(2,1)S(1)}, bf16[4,1024,256]{2,1,0:T(8,128)(2,1)}, u32[]{:S(2)}, u32[]{:S(2)}) collective-permute-start(bf16[4,1024,256]{2,1,0:T(8,128)(2,1)S(1)} %get-tuple-element.24.refs_0_), channel_id=1, source_target_pairs={{0,12},{1,13},{2,14},{3,15},{4,0},{5,1},{6,2},{7,3},{8,4},{9,5},{1... | collective-permute-start | bytes 6291464 | tf_op jit(solution)/shard_map/ppermute | solution.py:38
  23.2 31.9 %copy-start.4 = (s32[1024]{0:T(1024)S(1)}, s32[1024]{0:T(1024)}, u32[]{:S(2)}) copy-start(s32[1024]{0:T(1024)} %param.17) | copy-start | bytes 12292
  49.6 46.0 %collective-permute-start.4 = (bf16[2,1024,256]{2,1,0:T(8,128)(2,1)}, bf16[2,1024,256]{2,1,0:T(8,128)(2,1)}, u32[]{:S(2)}, u32[]{:S(2)}) collective-permute-start(bf16[2,1024,256]{2,1,0:T(8,128)(2,1)} %slice.40), channel_id=1, source_target_pairs={{0,4},{1,5},{2,6},{3,7},{4,8},{5,9},{6,10},{7,11},{8,12},{9,13},{1... | collective-permute-start | bytes 3145736 | tf_op jit(solution)/shard_map/ppermute | solution.py:38
  51.9 43.8 %collective-permute-start.6 = (bf16[2,1024,256]{2,1,0:T(8,128)(2,1)}, bf16[2,1024,256]{2,1,0:T(8,128)(2,1)}, u32[]{:S(2)}, u32[]{:S(2)}) collective-permute-start(bf16[2,1024,256]{2,1,0:T(8,128)(2,1)} %slice.41), channel_id=1, source_target_pairs={{0,12},{1,13},{2,14},{3,15},{4,0},{5,1},{6,2},{7,3},{8,4},{9,5},{1... | collective-permute-start | bytes 3145736 | tf_op jit(solution)/shard_map/ppermute | solution.py:38
  55.3 10.6 %collective-permute-start.7 = (f32[1024]{0:T(1024)S(1)}, f32[1024]{0:T(1024)S(1)}, u32[]{:S(2)}, u32[]{:S(2)}) collective-permute-start(f32[1024]{0:T(1024)S(1)} %get-tuple-element.23), channel_id=1, source_target_pairs={{0,4},{1,5},{2,6},{3,7},{4,8},{5,9},{6,10},{7,11},{8,12},{9,13},{1... | collective-permute-start | bytes 12296 | tf_op jit(solution)/shard_map/ppermute | solution.py:38
  55.4 12.4 %collective-permute-start.8 = (f32[1024]{0:T(1024)S(1)}, f32[1024]{0:T(1024)S(1)}, u32[]{:S(2)}, u32[]{:S(2)}) collective-permute-start(f32[1024]{0:T(1024)S(1)} %get-tuple-element.23), channel_id=1, source_target_pairs={{0,12},{1,13},{2,14},{3,15},{4,0},{5,1},{6,2},{7,3},{8,4},{9,5},{1... | collective-permute-start | bytes 12296 | tf_op jit(solution)/shard_map/ppermute | solution.py:38
  58.6 9.2 %collective-permute-start.9 = (f32[1024]{0:T(1024)S(1)}, f32[1024]{0:T(1024)S(1)}, u32[]{:S(2)}, u32[]{:S(2)}) collective-permute-start(f32[1024]{0:T(1024)S(1)} %get-tuple-element.23), channel_id=1, source_target_pairs={{0,8},{1,9},{2,10},{3,11},{4,12},{5,13},{6,14},{7,15},{8,0},{9,1},... | collective-permute-start | bytes 12296 | tf_op jit(solution)/shard_map/ppermute | solution.py:38
  107.7 1.9 collective-permute-start.11
  109.7 25.3 %collective-permute-start.12 = (bf16[2,1024,256]{2,1,0:T(8,128)(2,1)S(1)}, bf16[2,1024,256]{2,1,0:T(8,128)(2,1)S(1)}, u32[]{:S(2)}, u32[]{:S(2)}) collective-permute-start(bf16[2,1024,256]{2,1,0:T(8,128)(2,1)S(1)} %pad_maximum_fusion.1.kv_ref), channel_id=1, source_target_pairs={{0,32},{16,48},{32,64},{48,80},{64,96},{80,112},{96,0},{112,16},{1... | collective-permute-start | bytes 3145736 | tf_op jit(solution)/shard_map/ppermute | solution.py:43
  110.3 26.5 %collective-permute-start.13 = (bf16[2,1024,256]{2,1,0:T(8,128)(2,1)S(1)}, bf16[2,1024,256]{2,1,0:T(8,128)(2,1)S(1)}, u32[]{:S(2)}, u32[]{:S(2)}) collective-permute-start(bf16[2,1024,256]{2,1,0:T(8,128)(2,1)S(1)} %pad_maximum_fusion.1.kv_ref), channel_id=1, source_target_pairs={{0,96},{16,112},{32,0},{48,16},{64,32},{80,48},{96,64},{112,80},{1... | collective-permute-start | bytes 3145736 | tf_op jit(solution)/shard_map/ppermute | solution.py:43
  111.8 1.9 collective-permute-start.10
  135.0 55.1 %collective-permute-start.14 = (bf16[1,1024,256]{2,1,0:T(8,128)(2,1)S(1)}, bf16[1,1024,256]{2,1,0:T(8,128)(2,1)S(1)}, u32[]{:S(2)}, u32[]{:S(2)}) collective-permute-start(bf16[1,1024,256]{2,1,0:T(8,128)(2,1)S(1)} %slice.42), channel_id=1, source_target_pairs={{0,32},{16,48},{32,64},{48,80},{64,96},{80,112},{96,0},{112,16},{1... | collective-permute-start | bytes 1572872 | tf_op jit(solution)/shard_map/ppermute | solution.py:43
  136.8 53.3 %collective-permute-start.15 = (bf16[1,1024,256]{2,1,0:T(8,128)(2,1)S(1)}, bf16[1,1024,256]{2,1,0:T(8,128)(2,1)S(1)}, u32[]{:S(2)}, u32[]{:S(2)}) collective-permute-start(bf16[1,1024,256]{2,1,0:T(8,128)(2,1)S(1)} %slice.43), channel_id=1, source_target_pairs={{0,96},{16,112},{32,0},{48,16},{64,32},{80,48},{96,64},{112,80},{1... | collective-permute-start | bytes 1572872 | tf_op jit(solution)/shard_map/ppermute | solution.py:43
  144.1 1.3 copy-start.2
  215.4 1.6 collective-permute-start.16
  221.3 14.9 %collective-permute-start.19 = (bf16[2,1024,256]{2,1,0:T(8,128)(2,1)S(1)}, bf16[2,1024,256]{2,1,0:T(8,128)(2,1)S(1)}, u32[]{:S(2)}, u32[]{:S(2)}) collective-permute-start(bf16[2,1024,256]{2,1,0:T(8,128)(2,1)S(1)} %shard_map.161), channel_id=1, source_target_pairs={{0,3},{1,0},{2,1},{3,2},{4,7},{5,4},{6,5},{7,6},{8,11},{9,8},{10,9... | collective-permute-start | bytes 3145736 | tf_op jit(solution)/shard_map/ppermute | solution.py:38
  228.4 20.4 %collective-permute-start.17 = (bf16[2,1024,256]{2,1,0:T(8,128)(2,1)}, bf16[2,1024,256]{2,1,0:T(8,128)(2,1)}, u32[]{:S(2)}, u32[]{:S(2)}) collective-permute-start(bf16[2,1024,256]{2,1,0:T(8,128)(2,1)} %shard_map.159), channel_id=1, source_target_pairs={{0,1},{1,2},{2,3},{3,0},{4,5},{5,6},{6,7},{7,4},{8,9},{9,10},{10,1... | collective-permute-start | bytes 3145736 | tf_op jit(solution)/shard_map/ppermute | solution.py:38
  236.2 1.0 copy-start
  237.1 1.2 copy-start.1
  245.5 26.8 %collective-permute-start.20 = (bf16[4,1024,256]{2,1,0:T(8,128)(2,1)S(1)}, bf16[4,1024,256]{2,1,0:T(8,128)(2,1)}, u32[]{:S(2)}, u32[]{:S(2)}) collective-permute-start(bf16[4,1024,256]{2,1,0:T(8,128)(2,1)S(1)} %shard_map.162), channel_id=1, source_target_pairs={{0,3},{1,0},{2,1},{3,2},{4,7},{5,4},{6,5},{7,6},{8,11},{9,8},{10,9... | collective-permute-start | bytes 6291464 | tf_op jit(solution)/shard_map/ppermute | solution.py:38
  256.9 27.6 %collective-permute-start.18 = (bf16[4,1024,256]{2,1,0:T(8,128)(2,1)}, bf16[4,1024,256]{2,1,0:T(8,128)(2,1)}, u32[]{:S(2)}, u32[]{:S(2)}) collective-permute-start(bf16[4,1024,256]{2,1,0:T(8,128)(2,1)} %shard_map.160), channel_id=1, source_target_pairs={{0,1},{1,2},{2,3},{3,0},{4,5},{5,6},{6,7},{7,4},{8,9},{9,10},{10,1... | collective-permute-start | bytes 6291464 | tf_op jit(solution)/shard_map/ppermute | solution.py:38
  256.9 53.8 %copy-start.3 = (bf16[1024,256]{1,0:T(8,128)(2,1)S(1)}, bf16[1024,256]{1,0:T(8,128)(2,1)}, u32[]{:S(2)}) copy-start(bf16[1024,256]{1,0:T(8,128)(2,1)} %param.16) | copy-start | bytes 1572868
  292.7 10.9 %collective-permute-start.21 = (bf16[1024,256]{1,0:T(8,128)(2,1)S(1)}, bf16[1024,256]{1,0:T(8,128)(2,1)S(1)}, u32[]{:S(2)}, u32[]{:S(2)}) collective-permute-start(bf16[1024,256]{1,0:T(8,128)(2,1)S(1)} %get-tuple-element.18), channel_id=1, source_target_pairs={{0,4},{1,5},{2,6},{3,7},{4,8},{5,9},{6,10},{7,11},{8,12},{9,13},{1... | collective-permute-start | bytes 1572872 | tf_op jit(solution)/shard_map/ppermute | solution.py:38
  294.8 15.9 %collective-permute-start.22 = (bf16[1024,256]{1,0:T(8,128)(2,1)S(1)}, bf16[1024,256]{1,0:T(8,128)(2,1)S(1)}, u32[]{:S(2)}, u32[]{:S(2)}) collective-permute-start(bf16[1024,256]{1,0:T(8,128)(2,1)S(1)} %get-tuple-element.19), channel_id=1, source_target_pairs={{0,8},{1,9},{2,10},{3,11},{4,12},{5,13},{6,14},{7,15},{8,0},{9,1},... | collective-permute-start | bytes 1572872 | tf_op jit(solution)/shard_map/ppermute | solution.py:38
  297.9 12.8 %collective-permute-start.23 = (bf16[1024,256]{1,0:T(8,128)(2,1)S(1)}, bf16[1024,256]{1,0:T(8,128)(2,1)S(1)}, u32[]{:S(2)}, u32[]{:S(2)}) collective-permute-start(bf16[1024,256]{1,0:T(8,128)(2,1)S(1)} %get-tuple-element.20), channel_id=1, source_target_pairs={{0,12},{1,13},{2,14},{3,15},{4,0},{5,1},{6,2},{7,3},{8,4},{9,5},{1... | collective-permute-start | bytes 1572872 | tf_op jit(solution)/shard_map/ppermute | solution.py:38
